TPU v7x, 32 devices: a whole 2x2x4 slice. The times are simulated.
32 devices in a mesh: rep: 4 (over y, x), shard: 8 (over z, core).
Axes of the slice: x: 2, y: 2, z: 4, core: 2. Of those that a mesh axis runs over, the one named last changes fastest.
Arguments:
- tokens: bfloat16 [32768, 768], P(('rep', 'shard')), may hold values from -6 to 6
- cotangent: bfloat16 [32768, 768], P(('rep', 'shard')), may hold values from -6 to 6
- deletion: int32 [128, 256], P(('rep', 'shard')), may hold values 0 or 1
- lengths: int32 [128], P(('rep', 'shard')), may hold values from 64 to 256, as said below
- qkv_weight: float32 [768, 2304], P('shard'), may hold values from -0.21875 to 0.21875
- out_weight: float32 [768, 768], P('shard'), may hold values from -0.875 to 0.875
- up_weight: float32 [768, 3072], P('shard'), may hold values from -0.21875 to 0.21875
- down_weight: float32 [3072, 768], P('shard'), may hold values from -0.109375 to 0.109375
- vectors: float32 [12, 768], P(None, 'shard'), may hold values from -2 to 2
- qkv_first: float32 [768, 2304], P('shard'), may hold values from -192 to 192
- out_first: float32 [768, 768], P('shard'), may hold values from -192 to 192
- up_first: float32 [768, 3072], P('shard'), may hold values from -192 to 192
- down_first: float32 [3072, 768], P('shard'), may hold values from -192 to 192
- vector_first: float32 [12, 768], P(None, 'shard'), may hold values from -192 to 192
- qkv_second: float32 [768, 2304], P('shard'), may hold values from 10 to 100000
- out_second: float32 [768, 768], P('shard'), may hold values from 10 to 100000
- up_second: float32 [768, 3072], P('shard'), may hold values from 10 to 100000
- down_second: float32 [3072, 768], P('shard'), may hold values from 10 to 100000
- vector_second: float32 [12, 768], P(None, 'shard'), may hold values from 10 to 100000
Outputs:
- output: bfloat16 [32768, 768], P(('rep', 'shard'))
- token_grad: bfloat16 [32768, 768], P(('rep', 'shard'))
- qkv_grad: float32 [768, 2304], P('shard')
- out_grad: float32 [768, 768], P('shard')
- up_grad: float32 [768, 3072], P('shard')
- down_grad: float32 [3072, 768], P('shard')
- vector_grad: float32 [12, 768], P(None, 'shard')
- qkv_step: float32 [768, 2304], P('shard')
- out_step: float32 [768, 768], P('shard')
- up_step: float32 [768, 3072], P('shard')
- down_step: float32 [3072, 768], P('shard')
- vector_step: float32 [12, 768], P(None, 'shard')
- qkv_first_new: float32 [768, 2304], P('shard')
- out_first_new: float32 [768, 768], P('shard')
- up_first_new: float32 [768, 3072], P('shard')
- down_first_new: float32 [3072, 768], P('shard')
- vector_first_new: float32 [12, 768], P(None, 'shard')
Inputs may be any that keep to these rules, and one draw needn't show every extreme that they name: `lengths`: in every draw some crop has all 256 positions in use and another only 64.
All inputs are finite; a program needn't handle non-finite values. No bound on the sum of `deletion` on one device may be relied on, other than what follows from the above.
Results may differ from a plain program's by a relative error of at most 0.015.
The roundings to bfloat16 on the way count: a program that leaves them out, or rounds other values in their place, can miss the bound.
Values may be sent and summed in bfloat16 or wider, within the bound.
A program may use at most 256 MiB of HBM per device.

v0:
```python
from functools import partial
import math
import jax
import jax.numpy as jnp
from jax import lax
from jax.sharding import PartitionSpec as P

D = 768
H = 12
FF = 3072
CROP = 256
norm_epsilon = 1e-06
decay_first = 0.9
decay_second = 0.999
correct_first = 1.0 - 2.6561398887587544e-05
correct_second = 0.0952078528862904
adam_epsilon = 1e-08


def layer_norm(hidden, gain_row, shift_row):
    average = jnp.mean(hidden, axis=-1, keepdims=True)
    centred = hidden - average
    variance = jnp.mean(centred * centred, axis=-1, keepdims=True)
    inverse_root = lax.rsqrt(variance + norm_epsilon)
    normed = centred * inverse_root
    return (normed * gain_row + shift_row, normed, inverse_root)


def norm_back(grad_output, normed, inverse_root, gain_row):
    grad_normed = grad_output * gain_row
    grad_input = inverse_root * (
        grad_normed
        - jnp.mean(grad_normed, axis=-1, keepdims=True)
        - normed * jnp.mean(grad_normed * normed, axis=-1, keepdims=True)
    )
    return (grad_input, jnp.sum(grad_output * normed, axis=0), jnp.sum(grad_output, axis=0))


def attend_block(pieces):
    packed, allowed_block = pieces
    score_scale = 1.0 / math.sqrt(packed.shape[-1])
    queries = packed[:, :, 0]
    keys_in = packed[:, :, 1]
    values = packed[:, :, 2]
    scores = (
        jnp.einsum("clhd,cmhd->chlm", queries, keys_in, preferred_element_type=jnp.float32)
        * score_scale
    )
    scores = jnp.where(allowed_block[:, None, None, :], scores, -1e30)
    row_top = jnp.max(scores, axis=-1, keepdims=True)
    log_totals = row_top + jnp.log(jnp.sum(jnp.exp(scores - row_top), axis=-1, keepdims=True))
    probs_low = jnp.exp(scores - log_totals).astype(jnp.bfloat16)
    mixed_rows = jnp.einsum(
        "chlm,cmhd->clhd", probs_low, values, preferred_element_type=jnp.float32
    )
    return (mixed_rows, log_totals[..., 0])


def attend_back(pieces):
    packed, allowed_block, log_totals, grad_mixed = pieces
    score_scale = 1.0 / math.sqrt(packed.shape[-1])
    queries = packed[:, :, 0]
    keys_in = packed[:, :, 1]
    values = packed[:, :, 2]
    scores = (
        jnp.einsum("clhd,cmhd->chlm", queries, keys_in, preferred_element_type=jnp.float32)
        * score_scale
    )
    scores = jnp.where(allowed_block[:, None, None, :], scores, -1e30)
    soft_probs = jnp.exp(scores - log_totals[..., None])
    grad_probs = jnp.einsum(
        "clhd,cmhd->chlm", grad_mixed, values, preferred_element_type=jnp.float32
    )
    grad_values = jnp.einsum(
        "chlm,clhd->cmhd",
        soft_probs.astype(jnp.bfloat16),
        grad_mixed,
        preferred_element_type=jnp.float32,
    )
    grad_scores = soft_probs * (
        grad_probs - jnp.sum(grad_probs * soft_probs, axis=-1, keepdims=True)
    )
    grad_low = grad_scores.astype(jnp.bfloat16)
    grad_queries = (
        jnp.einsum("chlm,cmhd->clhd", grad_low, keys_in, preferred_element_type=jnp.float32)
        * score_scale
    )
    grad_keys = (
        jnp.einsum("chlm,clhd->cmhd", grad_low, queries, preferred_element_type=jnp.float32)
        * score_scale
    )
    return jnp.stack([grad_queries, grad_keys, grad_values], axis=2)


def adam_update(gradient, first_moment, second_moment):
    first_new = decay_first * first_moment + (1.0 - decay_first) * gradient
    second_new = decay_second * second_moment + (1.0 - decay_second) * gradient * gradient
    step_dir = first_new / correct_first / (jnp.sqrt(second_new / correct_second) + adam_epsilon)
    return (step_dir, first_new)


def per_device(
    tokens,
    cotangent,
    deletion,
    lengths,
    qkv_weight,
    out_weight,
    up_weight,
    down_weight,
    vectors,
    qkv_first,
    out_first,
    up_first,
    down_first,
    vector_first,
    qkv_second,
    out_second,
    up_second,
    down_second,
    vector_second,
):
    crop_count = lengths.shape[0]
    head_size = D // H
    qkv_low = qkv_weight.astype(jnp.bfloat16)
    out_low = out_weight.astype(jnp.bfloat16)
    up_low = up_weight.astype(jnp.bfloat16)
    down_low = down_weight.astype(jnp.bfloat16)
    vector_low = vectors.astype(jnp.bfloat16)
    gathered = (
        lax.all_gather(qkv_low, "shard", axis=0, tiled=True),
        lax.all_gather(out_low, "shard", axis=0, tiled=True),
        lax.all_gather(up_low, "shard", axis=0, tiled=True),
        lax.all_gather(down_low, "shard", axis=0, tiled=True),
        lax.all_gather(vector_low, "shard", axis=1, tiled=True),
    )
    qkv_full, out_full, up_full, down_full, vector_full = gathered
    vector_float = vector_full.astype(jnp.float32)
    places = jnp.arange(CROP, dtype=jnp.int32)[None, :]
    allowed = ((deletion == 1) | (places == 0)) & (places < lengths[:, None])
    block_crops = math.gcd(crop_count, max(1, 512 // CROP))
    block_count = crop_count // block_crops
    allowed_blocks = allowed.reshape(block_count, block_crops, CROP)
    qkv_bias = jnp.concatenate([vector_float[0], jnp.zeros((D,), jnp.float32), vector_float[1]])
    qkv_act = (jnp.dot(tokens, qkv_full, preferred_element_type=jnp.float32) + qkv_bias).astype(
        jnp.bfloat16
    )
    packed = qkv_act.reshape(block_count, block_crops, CROP, 3, H, head_size)
    mixed_rows, log_totals = lax.map(attend_block, (packed, allowed_blocks))
    mixed_low = mixed_rows.reshape(crop_count * CROP, D).astype(jnp.bfloat16)
    branch = jnp.dot(mixed_low, out_full, preferred_element_type=jnp.float32) + vector_float[2]
    first_out, first_normed, first_root = layer_norm(
        tokens.astype(jnp.float32) + branch, vector_float[3], vector_float[4]
    )
    first_low = first_out.astype(jnp.bfloat16)
    inner_act = jnp.dot(first_low, up_full, preferred_element_type=jnp.float32) + vector_float[
        5:9
    ].reshape(FF)
    activated, gelu_back = jax.vjp(partial(jax.nn.gelu, approximate=False), inner_act)
    act_low = activated.astype(jnp.bfloat16)
    second = jnp.dot(act_low, down_full, preferred_element_type=jnp.float32) + vector_float[9]
    result, second_normed, second_root = layer_norm(
        first_out + second, vector_float[10], vector_float[11]
    )
    output = result.astype(jnp.bfloat16)
    back_set = (
        lax.all_gather(qkv_low, "shard", axis=0, tiled=True),
        lax.all_gather(out_low, "shard", axis=0, tiled=True),
        lax.all_gather(up_low, "shard", axis=0, tiled=True),
        lax.all_gather(down_low, "shard", axis=0, tiled=True),
        lax.all_gather(vector_low, "shard", axis=1, tiled=True),
    )
    qkv_back, out_back, up_back, down_back, vector_back = back_set
    vector_again = vector_back.astype(jnp.float32)
    keep_rows = allowed.reshape(crop_count * CROP).astype(jnp.float32)
    grad_result = cotangent.astype(jnp.float32) * keep_rows[:, None]
    grad_sum2, second_gain_grad, second_shift_grad = norm_back(
        grad_result, second_normed, second_root, vector_again[10]
    )
    grad_second = grad_sum2.astype(jnp.bfloat16)
    down_bias_grad = jnp.sum(grad_second, axis=0, dtype=jnp.float32)
    grad_down = jnp.einsum("tf,td->fd", act_low, grad_second, preferred_element_type=jnp.float32)
    grad_act = jnp.einsum("td,fd->tf", grad_second, down_back, preferred_element_type=jnp.float32)
    grad_inner = gelu_back(grad_act)[0].astype(jnp.bfloat16)
    up_bias_grad = jnp.sum(grad_inner, axis=0, dtype=jnp.float32)
    grad_up = jnp.einsum("td,tf->df", first_low, grad_inner, preferred_element_type=jnp.float32)
    grad_first = grad_sum2 + jnp.einsum(
        "tf,df->td", grad_inner, up_back, preferred_element_type=jnp.float32
    )
    grad_sum1, first_gain_grad, first_shift_grad = norm_back(
        grad_first, first_normed, first_root, vector_again[3]
    )
    grad_branch = grad_sum1.astype(jnp.bfloat16)
    out_bias_grad = jnp.sum(grad_branch, axis=0, dtype=jnp.float32)
    grad_out = jnp.einsum("td,te->de", mixed_low, grad_branch, preferred_element_type=jnp.float32)
    grad_mixed = jnp.einsum(
        "te,de->td", grad_branch, out_back, preferred_element_type=jnp.float32
    ).astype(jnp.bfloat16)
    grad_blocks = grad_mixed.reshape(block_count, block_crops, CROP, H, head_size)
    grad_packed = lax.map(attend_back, (packed, allowed_blocks, log_totals, grad_blocks))
    grad_qkv = grad_packed.reshape(crop_count * CROP, 3 * D).astype(jnp.bfloat16)
    bias_sums = jnp.sum(grad_qkv, axis=0, dtype=jnp.float32)
    grad_qkv_weight = jnp.einsum("td,te->de", tokens, grad_qkv, preferred_element_type=jnp.float32)
    token_grad = (
        grad_sum1 + jnp.einsum("te,de->td", grad_qkv, qkv_back, preferred_element_type=jnp.float32)
    ).astype(jnp.bfloat16)
    grad_vectors = jnp.concatenate(
        [
            jnp.stack(
                [
                    bias_sums[:D],
                    bias_sums[2 * D :],
                    out_bias_grad,
                    first_gain_grad,
                    first_shift_grad,
                ]
            ),
            up_bias_grad.reshape(4, D),
            jnp.stack([down_bias_grad, second_gain_grad, second_shift_grad]),
        ],
        axis=0,
    )
    group_sums = (
        lax.psum_scatter(grad_qkv_weight, "shard", scatter_dimension=0, tiled=True),
        lax.psum_scatter(grad_out, "shard", scatter_dimension=0, tiled=True),
        lax.psum_scatter(grad_up, "shard", scatter_dimension=0, tiled=True),
        lax.psum_scatter(grad_down, "shard", scatter_dimension=0, tiled=True),
        lax.psum_scatter(grad_vectors, "shard", scatter_dimension=1, tiled=True),
    )
    gradients = (
        lax.psum(group_sums[0].astype(jnp.bfloat16), "rep").astype(jnp.float32),
        lax.psum(group_sums[1].astype(jnp.bfloat16), "rep").astype(jnp.float32),
        lax.psum(group_sums[2].astype(jnp.bfloat16), "rep").astype(jnp.float32),
        lax.psum(group_sums[3].astype(jnp.bfloat16), "rep").astype(jnp.float32),
        lax.psum(group_sums[4].astype(jnp.bfloat16), "rep").astype(jnp.float32),
    )
    firsts = (qkv_first, out_first, up_first, down_first, vector_first)
    seconds = (qkv_second, out_second, up_second, down_second, vector_second)
    updated = [
        adam_update(gradient, first_moment, second_moment)
        for gradient, first_moment, second_moment in zip(gradients, firsts, seconds)
    ]
    return (
        output,
        token_grad,
        gradients[0],
        gradients[1],
        gradients[2],
        gradients[3],
        gradients[4],
        updated[0][0],
        updated[1][0],
        updated[2][0],
        updated[3][0],
        updated[4][0],
        updated[0][1],
        updated[1][1],
        updated[2][1],
        updated[3][1],
        updated[4][1],
    )


def solution(mesh):
    placed = (
        P(("rep", "shard"), None),
        P(("rep", "shard"), None),
        P(("rep", "shard"), None),
        P(("rep", "shard")),
        P("shard", None),
        P("shard", None),
        P("shard", None),
        P("shard", None),
        P(None, "shard"),
        P("shard", None),
        P("shard", None),
        P("shard", None),
        P("shard", None),
        P(None, "shard"),
        P("shard", None),
        P("shard", None),
        P("shard", None),
        P("shard", None),
        P(None, "shard"),
    )
    return jax.shard_map(
        per_device,
        mesh=mesh,
        in_specs=placed,
        out_specs=(
            P(("rep", "shard"), None),
            P(("rep", "shard"), None),
            P("shard", None),
            P("shard", None),
            P("shard", None),
            P("shard", None),
            P(None, "shard"),
            P("shard", None),
            P("shard", None),
            P("shard", None),
            P("shard", None),
            P(None, "shard"),
            P("shard", None),
            P("shard", None),
            P("shard", None),
            P("shard", None),
            P(None, "shard"),
        ),
        check_vma=False,
    )
```

profile of v0, /device:TPU:0, one launch (start us, length us, event | category | flops | bytes accessed | tf_op | source)
XLA Modules:
  0.0 704.1 jit_solution(15059409197622101852)
XLA Ops:
  14.6 15.8 %all-gather = bf16[8,96,12]{1,2,0:T(8,128)(2,1)S(1)} all-gather(bf16[1,96,12]{1,2,0:T(8,128)(2,1)S(1)} %convert_bitcast_fusion.1), channel_id=1, replica_groups=mesh['rep'=4,'shard'=8] {'shard'}, dimensions={0}, use_global_device_ids=true | all-gather | bytes 20736 | tf_op jit(solution)/shard_map/all_gather | solution.py:135
  35.1 19.5 %all-gather.6.cloned.1.call-done = bf16[768,2304]{1,0:T(8,128)(2,1)} async-done(((bf16[96,2304]{1,0:T(8,128)(2,1)}), bf16[768,2304]{1,0:T(8,128)(2,1)}) %all-gather.6.cloned.1.call-update) | async-done | bytes 3538960 | tf_op jit(solution)/shard_map/all_gather | solution.py:131
  54.6 7.5 %add_convert_fusion.1 = bf16[1024,2304]{1,0:T(8,128)(2,1)} fusion(bf16[1024,768]{1,0:T(8,128)(2,1)S(1)} %copy-done.7, bf16[768,2304]{1,0:T(8,128)(2,1)} %all-gather.6.cloned.1.call-done, f32[2304]{0:T(1024)S(1)} %pad_maximum_fusion), kind=kOutput, calls=%fused_computation.65 | convolution fusion | flops 3628597248 | bytes 9839616 | tf_op jit(solution)/shard_map/dot_general | solution.py:145
  62.1 6.6 copy.109
  68.8 8.9 %reshape.144 = bf16[2,2,256,3,12,64]{2,1,0,5,4,3:T(2,128)(2,1)} reshape(bf16[1024,2304]{0,1:T(8,128)(2,1)} %copy.109) | data formatting | bytes 9437184 | tf_op jit(solution)/shard_map/reshape | solution.py:148
  77.7 5.5 copy.110
  83.2 12.7 %while.22 = (s32[]{:T(128)}, bf16[2,2,256,12,64]{2,4,3,1,0:T(8,128)(2,1)S(1)}, f32[2,2,12,256]{3,2,1,0:T(8,128)S(1)}, bf16[2,2,256,3,12,64]{2,5,4,1,3,0:T(8,128)...) while((s32[]{:T(128)}, bf16[2,2,256,12,64]{2,4,3,1,0:T(8,128)(2,1)S(1)}, f32[2,2,12,256]{3,2,1,0:T(8,128)S(1)}, ...), condition=%wide.region_3.4_spmd, body=%wide.region_0.3_spmd.sunk | while | flops 419948544 | bytes 27766356 | solution.py:149
  99.8 3.9 fusion.72
  104.1 28.0 %all-gather.10.cloned.1.call-done = bf16[768,3072]{1,0:T(8,128)(2,1)} async-done(((bf16[96,3072]{1,0:T(8,128)(2,1)}), bf16[768,3072]{1,0:T(8,128)(2,1)}) %all-gather.10.cloned.1.call-update) | async-done | bytes 4718608 | tf_op jit(solution)/shard_map/all_gather | solution.py:133
  132.2 37.8 %multiply_convert_fusion.1 = (bf16[1024,3072]{1,0:T(8,128)(2,1)}, f32[1024,3072]{1,0:T(8,128)}, f32[1024,3072]{1,0:T(8,128)}) fusion(f32[3072]{0:T(1024)S(1)} %add.200, bf16[768,3072]{1,0:T(8,128)(2,1)} %all-gather.10.cloned.1.call-done, f32[1024,768]{0,1:T(8,128)S(1)} %get-tuple-element.266, f32[768]{0:T(1024)S(1)} %get-tuple-element.203, ...), kind=kOutput, calls=%fused_computation.50 | convolution fusion | flops 5043388416 | bytes 39348224 | tf_op jit(solution)/shard_map/dot_general | solution.py:156
  169.9 14.8 %all-gather.12.cloned.1.call-done = bf16[3072,768]{1,0:T(8,128)(2,1)} async-done(((bf16[384,768]{1,0:T(8,128)(2,1)}), bf16[3072,768]{1,0:T(8,128)(2,1)}) %all-gather.12.cloned.1.call-update) | async-done | bytes 4718608 | tf_op jit(solution)/shard_map/all_gather | solution.py:134
  184.8 9.4 %fusion.73 = (f32[1024]{0:T(1024)S(1)}, f32[1024,768]{0,1:T(8,128)S(1)}) fusion(f32[768]{0:T(1024)S(1)} %copy-done.39, bf16[1024,3072]{1,0:T(8,128)(2,1)} %get-tuple-element.254, bf16[3072,768]{1,0:T(8,128)(2,1)} %all-gather.12.cloned.1.call-done, f32[768]{0:T(1024)S(1)} %get-tuple-element.203, f32[768]{0:T(1024)S(1)} %get-tuple-element.204, ...), kind=kOutput, calls=%fused_computation.158 | convolution fusion | flops 4837342208 | bytes 17323008 | tf_op jit(solution)/shard_map/dot_general | solution.py:161
  197.7 3.3 convert_reduce_fusion.2
  201.0 18.1 %convert_reduce_fusion = (f32[3072]{0:T(1024)}, bf16[1024,3072]{1,0:T(8,128)(2,1)}) fusion(f32[1024,3072]{1,0:T(8,128)} %get-tuple-element.255, bf16[1024,768]{0,1:T(8,128)(2,1)S(1)} %get-tuple-element.249, bf16[3072,768]{1,0:T(8,128)(2,1)} %all-gather.12.cloned.1.call-done, f32[1024,3072]{1,0:T(8,128)} %get-tuple-element.267, f32[3072]{0:T(1024)S(1)} %add.200), kind=kOutput, calls=%fused_computation.48 | convolution fusion | flops 4885312512 | bytes 37773312 | tf_op jit(solution)/shard_map/td,fd->tf/dot_general | solution.py:183
  219.1 11.2 %multiply_reduce_fusion.2 = (f32[768]{0:T(1024)S(1)}, f32[1024]{0:T(1024)S(1)}, f32[1024]{0:T(1024)S(1)}, f32[768]{0:T(1024)S(1)}, f32[1024,768]{0,1:T(8,128)S(1)}) fusion(f32[1024,768]{0,1:T(8,128)} %copy-done.1, f32[1024]{0:T(1024)S(1)} %add_rsqrt_fusion.1, f32[1024]{0:T(1024)S(1)} %broadcast_multiply_fusion.5, f32[768]{0:T(1024)S(1)} %get-tuple-element.204, ...), kind=kOutput, calls=%fused_computation.69 | convolution fusion | flops 4846776320 | bytes 22069248 | tf_op jit(solution)/shard_map/tf,df->td/dot_general | solution.py:187
  234.5 3.9 convolution_convert_fusion
  241.4 25.9 %while.23 = (s32[]{:T(128)}, bf16[2,2,256,3,12,64]{2,5,4,1,3,0:T(8,128)(2,1)}, bf16[2,2,256,3,12,64]{2,5,4,1,3,0:T(8,128)(2,1)}, pred[2,2,256]{2,1,0:T(4,128)(4,...) while((s32[]{:T(128)}, ...), condition=%wide.region_14.15_spmd, body=%wide.region_12.14_spmd.sunk | while | flops 1038870528 | bytes 66244188 | solution.py:200
  267.3 9.4 %copy.118 = bf16[2,2,256,3,12,64]{2,1,0,5,4,3:T(2,128)(2,1)} copy(bf16[2,2,256,3,12,64]{2,5,4,1,3,0:T(8,128)(2,1)} %get-tuple-element.79) | data formatting | bytes 9437184 | tf_op jit(solution)/shard_map/convert_element_type | solution.py:201
  276.7 8.8 %convert_element_type.148 = bf16[1024,2304]{0,1:T(8,128)(2,1)} reshape(bf16[2,2,256,3,12,64]{2,1,0,5,4,3:T(2,128)(2,1)} %copy.118) | data formatting | bytes 9437184 | tf_op jit(solution)/shard_map/convert_element_type | solution.py:201
  285.6 8.3 %convolution_bitcast_fusion = f32[768,2304]{0,1:T(8,128)} fusion(bf16[1024,2304]{0,1:T(8,128)(2,1)} %convert_element_type.148, bf16[1024,768]{1,0:T(8,128)(2,1)S(1)} %copy-done.8), kind=kOutput, calls=%fused_computation.66 | convolution fusion | flops 3623878656 | bytes 13369344 | tf_op jit(solution)/shard_map/td,te->de/dot_general | solution.py:203
  293.9 8.0 %copy.134 = f32[768,2304]{1,0:T(8,128)} copy(f32[768,2304]{0,1:T(8,128)} %convolution_bitcast_fusion) | data formatting | bytes 14155776
  303.3 10.1 %fusion.74 = f32[3072,768]{1,0:T(8,128)} fusion(bf16[1024,3072]{1,0:T(8,128)(2,1)} %get-tuple-element.254, bf16[1024,768]{0,1:T(8,128)(2,1)S(1)} %copy-done.12), kind=kOutput, calls=%fused_computation.159 | convolution fusion | flops 4831838208 | bytes 17301504 | tf_op jit(solution)/shard_map/tf,td->fd/dot_general | solution.py:182
  315.4 10.5 %fusion.64 = f32[768,3072]{1,0:T(8,128)} fusion(bf16[1024,3072]{1,0:T(8,128)(2,1)} %get-tuple-element.272, f32[1024,768]{0,1:T(8,128)S(1)} %copy-done.3, f32[768]{0:T(1024)S(1)} %copy-done.38, f32[768]{0:T(1024)S(1)} %get-tuple-element.204, f32[1024]{0:T(1024)S(1)} %add_rsqrt_fusion.1, f32[1024]{0:T(1024)S(1)} %broadcast_multiply_fusion.5), kind=kOutput, calls=%fused_computation.154 | convolution fusion | flops 4835770368 | bytes 18888704 | tf_op jit(solution)/shard_map/td,tf->df/dot_general | solution.py:186
  332.2 45.9 %reduce-scatter.16.cloned.1.call-done = f32[96,2304]{1,0:T(8,128)} async-done(((f32[768,2304]{1,0:T(8,128)}), f32[96,2304]{1,0:T(8,128)}) %reduce-scatter.16.cloned.1.call-update) | async-done | bytes 884752
  380.3 98.0 %reduce-scatter.14.cloned.1.call-done = f32[384,768]{1,0:T(8,128)} async-done(((f32[3072,768]{1,0:T(8,128)}), f32[384,768]{1,0:T(8,128)}) %reduce-scatter.14.cloned.1.call-update) | async-done | bytes 1179664 | tf_op jit(solution)/shard_map/reduce_scatter | solution.py:227
  480.4 98.1 %reduce-scatter.12.cloned.1.call-done = f32[96,3072]{1,0:T(8,128)} async-done(((f32[768,3072]{1,0:T(8,128)}), f32[96,3072]{1,0:T(8,128)}) %reduce-scatter.12.cloned.1.call-update) | async-done | bytes 1179664 | tf_op jit(solution)/shard_map/reduce_scatter | solution.py:226
  583.6 9.3 %add_convert_fusion.2 = bf16[1024,768]{0,1:T(8,128)(2,1)} fusion(f32[1024,768]{0,1:T(8,128)} %copy-done.5, bf16[768,2304]{1,0:T(8,128)(2,1)} %all-gather.6.cloned.1.call-done, bf16[1024,2304]{0,1:T(8,128)(2,1)} %convert_element_type.148), kind=kOutput, calls=%fused_computation.71 | convolution fusion | flops 3625451520 | bytes 12976128 | tf_op jit(solution)/shard_map/te,de->td/dot_general | solution.py:205
  597.2 13.2 %reduce-scatter.18.cloned.1.call-done = f32[96,12]{1,0:T(8,128)} async-done(((f32[768,12]{1,0:T(8,128)}), f32[96,12]{1,0:T(8,128)}) %reduce-scatter.18.cloned.1.call-update) | async-done | bytes 4624
  611.3 10.2 %psum.39 = bf16[12,96]{1,0:T(8,128)(2,1)S(1)} all-reduce(bf16[12,96]{1,0:T(8,128)(2,1)S(1)} %copy.137), channel_id=1, replica_groups=mesh['rep'=4,'shard'=8] {'rep'}, use_global_device_ids=true, to_apply=%region_32.33 | all-reduce | flops 1152 | bytes 4608 | tf_op jit(solution)/shard_map/psum | solution.py:235
  622.1 58.8 %all-reduce.3.cloned.1.call-done = (bf16[96,2304]{0,1:T(8,128)(2,1)}, bf16[96,768]{1,0:T(8,128)(2,1)}, bf16[96,3072]{1,0:T(8,128)(2,1)}, bf16[384,768]{1,0:T(8,128)(2,1)}) async-done(((bf16[96,2304]{0,1:T(8,128)(2,1)}, bf16[96,768]{1,0:T(8,128)(2,1)}, bf16[96,3072]{1,0:T(8,128)(2,1)}, bf16[384,768]{1,0:T(8,128)(2,1)}), (bf16[96,2304]{0,1:T(8,128)(2,1)}, bf16[96,768]{1,0:T(8,128)(2,1)}, ...) | async-done | bytes 1769488 | tf_op jit(solution)/shard_map/psum | solution.py:231
  683.1 3.2 multiply_add_fusion.3
  690.3 3.3 fusion.48
  (205 shorter events, 99.1 us)
Async XLA Ops:
  7.2 4.0 copy-start.17
  7.2 47.4 %all-gather.6.cloned.1.call-start = ((), (), s32[]{:S(2)}) async-start(), calls=%async_computation.5 | async-start | bytes 3981312 | tf_op jit(solution)/shard_map/all_gather | solution.py:131
  9.3 5.2 copy-start.34
  9.3 21.8 %copy-start.40 = (s32[4,256]{1,0:T(4,128)S(1)}, s32[4,256]{1,0:T(4,128)}, u32[]{:S(2)}) copy-start(s32[4,256]{1,0:T(4,128)} %param.25) | copy-start | bytes 12292
  9.3 21.8 %copy-start.41 = (s32[4]{0:T(128)S(1)}, s32[4]{0:T(128)}, u32[]{:S(2)}) copy-start(s32[4]{0:T(128)} %param.26) | copy-start | bytes 52
  9.3 21.9 %copy-start.7 = (bf16[1024,768]{1,0:T(8,128)(2,1)S(1)}, bf16[1024,768]{1,0:T(8,128)(2,1)}, u32[]{:S(2)}) copy-start(bf16[1024,768]{1,0:T(8,128)(2,1)} %param.23) | copy-start | bytes 4718596
  9.3 90.5 %all-gather.8.cloned.1.call-start = ((), (), s32[]{:S(2)}) async-start(), calls=%async_computation.6 | async-start | bytes 1327104 | tf_op jit(solution)/shard_map/all_gather | solution.py:132
  11.2 121.0 %all-gather.10.cloned.1.call-start = ((), (), s32[]{:S(2)}) async-start(), calls=%async_computation.7 | async-start | bytes 5308416 | tf_op jit(solution)/shard_map/all_gather | solution.py:133
  12.1 21.4 %copy-start.6 = (bf16[1024,768]{1,0:T(8,128)(2,1)S(1)}, bf16[1024,768]{1,0:T(8,128)(2,1)}, u32[]{:S(2)}) copy-start(bf16[1024,768]{1,0:T(8,128)(2,1)} %param.24) | copy-start | bytes 4718596
  12.1 172.7 %all-gather.12.cloned.1.call-start = ((), (), s32[]{:S(2)}) async-start(), calls=%async_computation.8 | async-start | bytes 5308416 | tf_op jit(solution)/shard_map/all_gather | solution.py:134
  14.5 316.1 %reduce-scatter.10.cloned.1.call-start = ((), (), s32[]{:S(2)}) async-start(), calls=%async_computation.9 | async-start | bytes 2654208 | tf_op jit(solution)/shard_map/reduce_scatter | solution.py:225
  31.1 153.7 %copy-start.37 = (f32[768]{0:T(1024)}, f32[768]{0:T(1024)S(1)}, u32[]{:S(2)}) copy-start(f32[768]{0:T(1024)S(1)} %get-tuple-element.203) | copy-start | bytes 9220
  77.7 5.5 copy-start.10
  95.8 4.0 copy-start.20
  95.8 4.0 copy-start.25
  103.7 81.1 %copy-start.1 = (f32[1024,768]{0,1:T(8,128)}, f32[1024,768]{0,1:T(8,128)S(1)}, u32[]{:S(2)}) copy-start(f32[1024,768]{0,1:T(8,128)S(1)} %get-tuple-element.266) | copy-start | bytes 9437188
  132.2 52.6 %copy-start.39 = (f32[768]{0:T(1024)S(1)}, f32[768]{0:T(1024)}, u32[]{:S(2)}) copy-start(f32[768]{0:T(1024)} %get-tuple-element.202) | copy-start | bytes 9220
  201.0 18.1 %copy-start.11 = (bf16[1024,768]{0,1:T(8,128)(2,1)}, bf16[1024,768]{0,1:T(8,128)(2,1)S(1)}, u32[]{:S(2)}) copy-start(bf16[1024,768]{0,1:T(8,128)(2,1)S(1)} %get-tuple-element.249) | copy-start | bytes 4718596
  219.1 11.2 %copy-start.2 = (f32[1024,768]{0,1:T(8,128)S(1)}, f32[1024,768]{0,1:T(8,128)}, u32[]{:S(2)}) copy-start(f32[1024,768]{0,1:T(8,128)} %copy-done.1) | copy-start | bytes 9437188
  241.4 136.7 %reduce-scatter.16.cloned.1.call-start = ((), (), s32[]{:S(2)}) async-start(), calls=%async_computation.12 | async-start | bytes 7962624
  276.7 8.8 %copy-start.8 = (bf16[1024,768]{1,0:T(8,128)(2,1)S(1)}, bf16[1024,768]{1,0:T(8,128)(2,1)}, u32[]{:S(2)}) copy-start(bf16[1024,768]{1,0:T(8,128)(2,1)} %param.23) | copy-start | bytes 4718596
  301.9 176.4 %reduce-scatter.14.cloned.1.call-start = ((), (), s32[]{:S(2)}) async-start(), calls=%async_computation.11 | async-start | bytes 10616832 | tf_op jit(solution)/shard_map/reduce_scatter | solution.py:227
  313.4 265.1 %reduce-scatter.12.cloned.1.call-start = ((), (), s32[]{:S(2)}) async-start(), calls=%async_computation.10 | async-start | bytes 10616832 | tf_op jit(solution)/shard_map/reduce_scatter | solution.py:226
  326.0 3.3 copy-start.31
  326.0 3.3 copy-start.30
  326.0 284.4 %reduce-scatter.18.cloned.1.call-start = ((), (), s32[]{:S(2)}) async-start(), calls=%async_computation.13 | async-start | bytes 442368
  330.5 350.4 %all-reduce.3.cloned.1.call-start = ((), (), s32[]{:S(2)}) async-start(), calls=%async_computation.14 | async-start | bytes 3833856 | tf_op jit(solution)/shard_map/psum | solution.py:231
  332.2 248.5 %copy-start.18 = (f32[96,2304]{1,0:T(8,128)S(1)}, f32[96,2304]{1,0:T(8,128)}, u32[]{:S(2)}) copy-start(f32[96,2304]{1,0:T(8,128)} %param.32) | copy-start | bytes 2654212
  593.0 28.5 %copy-start.35 = (f32[12,96]{1,0:T(8,128)S(1)}, f32[12,96]{1,0:T(8,128)}, u32[]{:S(2)}) copy-start(f32[12,96]{1,0:T(8,128)} %param.41) | copy-start | bytes 13828
  593.0 28.5 %copy-start.36 = (f32[12,96]{1,0:T(8,128)S(1)}, f32[12,96]{1,0:T(8,128)}, u32[]{:S(2)}) copy-start(f32[12,96]{1,0:T(8,128)} %param.36) | copy-start | bytes 13828
  686.3 4.0 copy-start.13
  686.3 4.0 copy-start.14
  (20 other events, 45.4 us)
Sparse Core Ops, SparseCore 0:
  10.2 44.3 all-gather.5
  56.8 21.5 all-gather.7
  80.7 51.4 all-gather.9
  134.2 50.5 all-gather.11
  241.5 35.2 reduce-scatter.9
  302.0 76.0 reduce-scatter.15
  380.4 97.8 reduce-scatter.13
  480.6 97.8 reduce-scatter.11
  581.3 29.0 reduce-scatter.17
  615.3 65.5 all-reduce.2
where the time goes:
time: 715 us; the launch traced here: 704 us
  waiting for transfers between devices  376 us (53%)
  matrix products  152 us (21%)
  local copies, waits for them, and re-layouts  89.8 us (13%)
  other arithmetic  43.7 us (6%)
  blocking collectives  26 us (4%)
  between operations  15.2 us (2%)
    reduce_scatter x1, waiting for transfers between devices, per_device(): lax.psum_scatter(grad_up, 'shard', scatter_dimension=0, tiled=True)  98.1 us
    reduce_scatter x1, waiting for transfers between devices, per_device(): lax.psum_scatter(grad_down, 'shard', scatter_dimension=0, tiled=True)  98 us
    unnamed x12, waiting for transfers between devices  59.3 us
    psum x1, waiting for transfers between devices, per_device(): lax.psum(group_sums[0].astype(jnp.bfloat16), 'rep').astype(jnp.float32)  58.8 us
    dot_general x1, matrix products, per_device(): jnp.dot(first_low, up_full, preferred_element_type=jnp.float32)  37.8 us
    unnamed x98, local copies, waits for them, and re-layouts  33.9 us
    all_gather x1, waiting for transfers between devices, per_device(): lax.all_gather(up_low, 'shard', axis=0, tiled=True)  28 us
    all_gather x1, waiting for transfers between devices, per_device(): lax.all_gather(qkv_low, 'shard', axis=0, tiled=True)  19.5 us
  transfers between devices with their start and end apart: 10, of which 8 were waited for; matrix products, arithmetic and copies ran while one was open for 30% of the time, Pallas kernels for 0%

commit v1 on v0

--- a/solution.py
+++ b/solution.py
@@ -15,6 +15,27 @@
 correct_first = 1.0 - 2.6561398887587544e-05
 correct_second = 0.0952078528862904
 adam_epsilon = 1e-08
+
+
+def _review_blocks(t0):
+    v1, finding, next_value = (lax.axis_size("shard"), lax.axis_index("shard"), t0.shape[0])
+    cards = tuple(((s, (s + 1) % v1) for s in range(v1)))
+    views = tuple(((s, (s - 1) % v1) for s in range(v1)))
+    opened = jnp.zeros((*t0.shape[:0], v1 * next_value, *t0.shape[1:]), t0.dtype)
+    earlier = e_now = t0
+    state_next = v1 // 2
+    opened = lax.dynamic_update_slice_in_dim(opened, t0, finding * next_value, axis=0)
+    for m in range(1, state_next + 1):
+        earlier = lax.ppermute(earlier, "shard", cards)
+        opened = lax.dynamic_update_slice_in_dim(
+            opened, earlier, (finding - m) % v1 * next_value, axis=0
+        )
+        if m < v1 - state_next:
+            e_now = lax.ppermute(e_now, "shard", views)
+            opened = lax.dynamic_update_slice_in_dim(
+                opened, e_now, (finding + m) % v1 * next_value, axis=0
+            )
+    return opened
 
 
 def layer_norm(hidden, gain_row, shift_row):
@@ -128,7 +149,7 @@
     down_low = down_weight.astype(jnp.bfloat16)
     vector_low = vectors.astype(jnp.bfloat16)
     gathered = (
-        lax.all_gather(qkv_low, "shard", axis=0, tiled=True),
+        _review_blocks(qkv_low),
         lax.all_gather(out_low, "shard", axis=0, tiled=True),
         lax.all_gather(up_low, "shard", axis=0, tiled=True),
         lax.all_gather(down_low, "shard", axis=0, tiled=True),

time: 715 us -> 767 us (1.073)
  waiting for transfers between devices: 376 us -> 406 us
  starting transfers between devices: 0.41 us -> 12.2 us
  blocking collectives: 26 us -> 35.9 us
    ppermute x0 -> x7, waiting for transfers between devices: none -> 47.2 us  [the longest x4 45.3 us: _review_blocks(): earlier = lax.ppermute(earlier, 'shard', cards)]
    all_gather x1, waiting for transfers between devices: 28 us -> 0.02 us  [per_device(): lax.all_gather(up_low, 'shard', axis=0, tiled=True)]
    all_gather x1, waiting for transfers between devices: 19.5 us -> 37 us  [per_device(): lax.all_gather(qkv_low, 'shard', axis=0, tiled=True)]
    all_gather x1, waiting for transfers between devices: 14.8 us -> 0.01 us  [per_device(): lax.all_gather(down_low, 'shard', axis=0, tiled=True)]
    ppermute x0 -> x7, starting transfers between devices: none -> 11.8 us  [the longest x3 10.8 us: _review_blocks(): e_now = lax.ppermute(e_now, 'shard', views)]
    all_gather x1, blocking collectives: 15.8 us -> 25.6 us  [per_device(): lax.all_gather(vector_low, 'shard', axis=1, tiled=True)]
    unnamed x12, waiting for transfers between devices: 59.3 us -> 67.1 us
    unnamed x98 -> x96, local copies, waits for them, and re-layouts: 33.9 us -> 37.8 us
  transfers between devices with their start and end apart: 10 -> 17, of which waited for: 8 -> 10; matrix products, arithmetic and copies ran while one was open for 30% -> 28% of each run, Pallas kernels for 0% -> 0%
where the time goes in v1:
time: 767 us; the launch traced here: 762 us
  waiting for transfers between devices  406 us (53%)
  matrix products  151 us (20%)
  local copies, waits for them, and re-layouts  93.4 us (12%)
  other arithmetic  47.2 us (6%)
  blocking collectives  35.9 us (5%)
  between operations  15.4 us (2%)
  starting transfers between devices  12.2 us (2%)
    reduce_scatter x1, waiting for transfers between devices, per_device(): lax.psum_scatter(grad_up, 'shard', scatter_dimension=0, tiled=True)  98.1 us
    reduce_scatter x1, waiting for transfers between devices, per_device(): lax.psum_scatter(grad_down, 'shard', scatter_dimension=0, tiled=True)  97.8 us
    unnamed x12, waiting for transfers between devices  67.1 us
    psum x1, waiting for transfers between devices, per_device(): lax.psum(group_sums[0].astype(jnp.bfloat16), 'rep').astype(jnp.float32)  58.8 us
    ppermute x4, waiting for transfers between devices, _review_blocks(): earlier = lax.ppermute(earlier, 'shard', cards)  45.3 us
    dot_general x1, matrix products, per_device(): jnp.dot(first_low, up_full, preferred_element_type=jnp.float32)  38.1 us
    unnamed x96, local copies, waits for them, and re-layouts  37.8 us
    all_gather x1, waiting for transfers between devices, per_device(): lax.all_gather(qkv_low, 'shard', axis=0, tiled=True)  37 us
  transfers between devices with their start and end apart: 17, of which 10 were waited for; matrix products, arithmetic and copies ran while one was open for 28% of the time, Pallas kernels for 0%

profile of v1, /device:TPU:0, one launch (start us, length us, event | category | flops | bytes accessed | tf_op | source)
XLA Modules:
  0.0 761.7 jit_solution(12635229544237813118)
XLA Ops:
  13.6 4.0 collective-permute-start.1
  20.5 25.6 %all-gather = bf16[8,96,12]{1,2,0:T(8,128)(2,1)S(1)} all-gather(bf16[1,96,12]{1,2,0:T(8,128)(2,1)S(1)} %convert_bitcast_fusion.1), channel_id=1, replica_groups=mesh['rep'=4,'shard'=8] {'shard'}, dimensions={0}, use_global_device_ids=true | all-gather | bytes 20736 | tf_op jit(solution)/shard_map/all_gather | solution.py:156
  65.0 17.8 %collective-permute-done.2 = bf16[96,2304]{1,0:T(8,128)(2,1)S(1)} collective-permute-done((bf16[96,2304]{1,0:T(8,128)(2,1)}, bf16[96,2304]{1,0:T(8,128)(2,1)S(1)}, u32[]{:S(2)}, u32[]{:S(2)}) %collective-permute-start.2) | collective-permute-done | bytes 442400 | tf_op jit(solution)/shard_map/ppermute | solution.py:29
  82.9 3.5 collective-permute-start.5
  86.5 16.8 %collective-permute-done.4 = bf16[96,2304]{1,0:T(8,128)(2,1)S(1)} collective-permute-done((bf16[96,2304]{1,0:T(8,128)(2,1)S(1)}, bf16[96,2304]{1,0:T(8,128)(2,1)S(1)}, u32[]{:S(2)}, u32[]{:S(2)}) %collective-permute-start.4) | collective-permute-done | bytes 442400 | tf_op jit(solution)/shard_map/ppermute | solution.py:29
  105.4 10.7 %collective-permute-done.6 = bf16[96,2304]{1,0:T(8,128)(2,1)S(1)} collective-permute-done((bf16[96,2304]{1,0:T(8,128)(2,1)S(1)}, bf16[96,2304]{1,0:T(8,128)(2,1)S(1)}, u32[]{:S(2)}, u32[]{:S(2)}) %collective-permute-start.6) | collective-permute-done | bytes 442400 | tf_op jit(solution)/shard_map/ppermute | solution.py:29
  116.2 6.2 fusion.30
  122.4 8.9 %reshape.144 = bf16[2,2,256,3,12,64]{2,1,0,5,4,3:T(2,128)(2,1)} reshape(bf16[1024,2304]{0,1:T(8,128)(2,1)} %fusion.30) | data formatting | bytes 9437184 | tf_op jit(solution)/shard_map/reshape | solution.py:169
  131.2 5.5 copy.107
  136.7 13.9 %while.22 = (s32[]{:T(128)}, bf16[2,2,256,12,64]{2,4,3,1,0:T(8,128)(2,1)S(1)}, f32[2,2,12,256]{3,2,1,0:T(8,128)}, bf16[2,2,256,3,12,64]{2,5,4,1,3,0:T(8,128)(2,1)}, pred[2,2,256]{2,1,0:T(4,128)(4,1)S(1)}, /*index=5*/s32[]{:T(128)}) while((s32[]{:T(128)}, bf16[2,2,256,12,64]{2,4,3,1,0:T(8,128)(2,1)S(1)}, f32[2,2,12,256]{3,2,1,0:T(8,128)}, ...), condition=%wide.region_3.4_spmd, body=%wide.region_0.3_spmd.sunk | while | flops 419948544 | bytes 27742288 | solution.py:170
  154.7 3.9 fusion.73
  159.3 38.1 %multiply_convert_fusion.1 = (bf16[1024,3072]{1,0:T(8,128)(2,1)}, f32[1024,3072]{1,0:T(8,128)}, f32[1024,3072]{1,0:T(8,128)}) fusion(f32[3072]{0:T(1024)S(1)} %copy-done.31, bf16[768,3072]{1,0:T(8,128)(2,1)} %all-gather.8.cloned.1.call-done, f32[1024,768]{0,1:T(8,128)S(1)} %get-tuple-element.268, f32[768]{0:T(1024)S(1)} %get-tuple-element.203, ...), kind=kOutput, calls=%fused_computation.50 | convolution fusion | flops 5043388416 | bytes 39348224 | tf_op jit(solution)/shard_map/dot_general | solution.py:177
  197.4 9.4 %fusion.74 = (f32[1024]{0:T(1024)S(1)}, f32[1024,768]{0,1:T(8,128)S(1)}) fusion(f32[768]{0:T(1024)S(1)} %get-tuple-element.202, bf16[1024,3072]{1,0:T(8,128)(2,1)} %get-tuple-element.254, bf16[3072,768]{1,0:T(8,128)(2,1)} %all-gather.10.cloned.1.call-done, f32[768]{0:T(1024)S(1)} %get-tuple-element.203, f32[768]{0:T(1024)S(1)} %get-tuple-element.204, ...), kind=kOutput, calls=%fused_computation.167 | convolution fusion | flops 4837342208 | bytes 17323008 | tf_op jit(solution)/shard_map/dot_general | solution.py:182
  210.3 3.3 convert_reduce_fusion.2
  213.6 18.1 %convert_reduce_fusion = (f32[3072]{0:T(1024)}, bf16[1024,3072]{1,0:T(8,128)(2,1)}) fusion(f32[1024,3072]{1,0:T(8,128)} %get-tuple-element.255, bf16[1024,768]{0,1:T(8,128)(2,1)S(1)} %get-tuple-element.249, bf16[3072,768]{1,0:T(8,128)(2,1)} %all-gather.10.cloned.1.call-done, f32[1024,3072]{1,0:T(8,128)} %get-tuple-element.269, f32[3072]{0:T(1024)S(1)} %copy-done.31), kind=kOutput, calls=%fused_computation.48 | convolution fusion | flops 4885312512 | bytes 37773312 | tf_op jit(solution)/shard_map/td,fd->tf/dot_general | solution.py:204
  231.7 11.2 %multiply_reduce_fusion.2 = (f32[768]{0:T(1024)S(1)}, f32[1024]{0:T(1024)S(1)}, f32[1024]{0:T(1024)S(1)}, f32[768]{0:T(1024)S(1)}, f32[1024,768]{0,1:T(8,128)S(1)}) fusion(f32[1024,768]{0,1:T(8,128)} %copy-done.1, f32[1024]{0:T(1024)S(1)} %add_rsqrt_fusion.1, f32[1024]{0:T(1024)S(1)} %broadcast_multiply_fusion.5, f32[768]{0:T(1024)S(1)} %get-tuple-element.204, ...), kind=kOutput, calls=%fused_computation.70 | convolution fusion | flops 4846776320 | bytes 22069248 | tf_op jit(solution)/shard_map/tf,df->td/dot_general | solution.py:208
  247.2 3.9 convolution_convert_fusion
  254.1 25.9 %while.23 = (s32[]{:T(128)}, bf16[2,2,256,3,12,64]{2,5,4,1,3,0:T(8,128)(2,1)}, bf16[2,2,256,3,12,64]{2,5,4,1,3,0:T(8,128)(2,1)}, pred[2,2,256]{2,1,0:T(4,128)(4,...) while((s32[]{:T(128)}, ...), condition=%wide.region_14.15_spmd, body=%wide.region_12.14_spmd.sunk | while | flops 1038870528 | bytes 66244188 | solution.py:221
  280.0 9.4 %copy.115 = bf16[2,2,256,3,12,64]{2,1,0,5,4,3:T(2,128)(2,1)} copy(bf16[2,2,256,3,12,64]{2,5,4,1,3,0:T(8,128)(2,1)} %get-tuple-element.79) | data formatting | bytes 9437184 | tf_op jit(solution)/shard_map/convert_element_type | solution.py:222
  289.4 8.8 %convert_element_type.152 = bf16[1024,2304]{0,1:T(8,128)(2,1)} reshape(bf16[2,2,256,3,12,64]{2,1,0,5,4,3:T(2,128)(2,1)} %copy.115) | data formatting | bytes 9437184 | tf_op jit(solution)/shard_map/convert_element_type | solution.py:222
  298.2 8.4 %convolution_bitcast_fusion = f32[768,2304]{0,1:T(8,128)} fusion(bf16[1024,2304]{0,1:T(8,128)(2,1)} %convert_element_type.152, bf16[1024,768]{1,0:T(8,128)(2,1)S(1)} %copy-done.7), kind=kOutput, calls=%fused_computation.66 | convolution fusion | flops 3623878656 | bytes 13369344 | tf_op jit(solution)/shard_map/td,te->de/dot_general | solution.py:224
  306.6 8.0 %copy.131 = f32[768,2304]{1,0:T(8,128)} copy(f32[768,2304]{0,1:T(8,128)} %convolution_bitcast_fusion) | data formatting | bytes 14155776
  316.0 10.2 %fusion.75 = f32[3072,768]{1,0:T(8,128)} fusion(bf16[1024,3072]{1,0:T(8,128)(2,1)} %get-tuple-element.254, bf16[1024,768]{0,1:T(8,128)(2,1)S(1)} %copy-done.11), kind=kOutput, calls=%fused_computation.168 | convolution fusion | flops 4831838208 | bytes 17301504 | tf_op jit(solution)/shard_map/tf,td->fd/dot_general | solution.py:203
  328.1 10.5 %fusion.65 = f32[768,3072]{1,0:T(8,128)} fusion(bf16[1024,3072]{1,0:T(8,128)(2,1)} %get-tuple-element.274, f32[1024,768]{0,1:T(8,128)S(1)} %copy-done.3, f32[768]{0:T(1024)S(1)} %copy-done.37, f32[768]{0:T(1024)S(1)} %get-tuple-element.204, f32[1024]{0:T(1024)S(1)} %add_rsqrt_fusion.1, f32[1024]{0:T(1024)S(1)} %broadcast_multiply_fusion.5), kind=kOutput, calls=%fused_computation.163 | convolution fusion | flops 4835770368 | bytes 18888704 | tf_op jit(solution)/shard_map/td,tf->df/dot_general | solution.py:207
  345.7 47.4 %reduce-scatter.16.cloned.1.call-done = f32[96,2304]{1,0:T(8,128)} async-done(((f32[768,2304]{1,0:T(8,128)}), f32[96,2304]{1,0:T(8,128)}) %reduce-scatter.16.cloned.1.call-update) | async-done | bytes 884752
  395.4 97.8 %reduce-scatter.14.cloned.1.call-done = f32[384,768]{1,0:T(8,128)} async-done(((f32[3072,768]{1,0:T(8,128)}), f32[384,768]{1,0:T(8,128)}) %reduce-scatter.14.cloned.1.call-update) | async-done | bytes 1179664 | tf_op jit(solution)/shard_map/reduce_scatter | solution.py:248
  495.3 98.1 %reduce-scatter.12.cloned.1.call-done = f32[96,3072]{1,0:T(8,128)} async-done(((f32[768,3072]{1,0:T(8,128)}), f32[96,3072]{1,0:T(8,128)}) %reduce-scatter.12.cloned.1.call-update) | async-done | bytes 1179664 | tf_op jit(solution)/shard_map/reduce_scatter | solution.py:247
  598.5 37.0 %all-gather.12.cloned.1.call-done = bf16[768,2304]{1,0:T(8,128)(2,1)} async-done(((bf16[96,2304]{1,0:T(8,128)(2,1)}), bf16[768,2304]{1,0:T(8,128)(2,1)}) %all-gather.12.cloned.1.call-update) | async-done | bytes 3538960 | tf_op jit(solution)/shard_map/all_gather | solution.py:188
  635.5 9.3 %add_convert_fusion.2 = bf16[1024,768]{0,1:T(8,128)(2,1)} fusion(f32[1024,768]{0,1:T(8,128)} %copy-done.5, bf16[768,2304]{1,0:T(8,128)(2,1)} %all-gather.12.cloned.1.call-done, bf16[1024,2304]{0,1:T(8,128)(2,1)} %convert_element_type.152), kind=kOutput, calls=%fused_computation.72 | convolution fusion | flops 3625451520 | bytes 12976128 | tf_op jit(solution)/shard_map/te,de->td/dot_general | solution.py:226
  649.1 18.8 %reduce-scatter.18.cloned.1.call-done = f32[96,12]{1,0:T(8,128)} async-done(((f32[768,12]{1,0:T(8,128)}), f32[96,12]{1,0:T(8,128)}) %reduce-scatter.18.cloned.1.call-update) | async-done | bytes 4624
  668.8 10.3 %psum.39 = bf16[12,96]{1,0:T(8,128)(2,1)S(1)} all-reduce(bf16[12,96]{1,0:T(8,128)(2,1)S(1)} %copy.134), channel_id=1, replica_groups=mesh['rep'=4,'shard'=8] {'rep'}, use_global_device_ids=true, to_apply=%region_32.33 | all-reduce | flops 1152 | bytes 4608 | tf_op jit(solution)/shard_map/psum | solution.py:256
  679.7 58.8 %all-reduce.3.cloned.1.call-done = (bf16[96,2304]{0,1:T(8,128)(2,1)}, bf16[96,768]{1,0:T(8,128)(2,1)}, bf16[96,3072]{1,0:T(8,128)(2,1)}, bf16[384,768]{1,0:T(8,128)(2,1)}) async-done(((bf16[96,2304]{0,1:T(8,128)(2,1)}, bf16[96,768]{1,0:T(8,128)(2,1)}, bf16[96,3072]{1,0:T(8,128)(2,1)}, bf16[384,768]{1,0:T(8,128)(2,1)}), (bf16[96,2304]{0,1:T(8,128)(2,1)}, bf16[96,768]{1,0:T(8,128)(2,1)}, ...) | async-done | bytes 1769488 | tf_op jit(solution)/shard_map/psum | solution.py:252
  (224 shorter events, 126.2 us)
Async XLA Ops:
  7.2 147.5 %all-gather.6.cloned.1.call-start = ((), (), s32[]{:S(2)}) async-start(), calls=%async_computation.5 | async-start | bytes 1327104 | tf_op jit(solution)/shard_map/all_gather | solution.py:153
  8.9 150.1 %all-gather.8.cloned.1.call-start = ((), (), s32[]{:S(2)}) async-start(), calls=%async_computation.6 | async-start | bytes 5308416 | tf_op jit(solution)/shard_map/all_gather | solution.py:154
  11.1 186.2 %all-gather.10.cloned.1.call-start = ((), (), s32[]{:S(2)}) async-start(), calls=%async_computation.7 | async-start | bytes 5308416 | tf_op jit(solution)/shard_map/all_gather | solution.py:155
  11.2 9.3 %copy-start.33 = (f32[12,96]{1,0:T(8,128)S(1)}, f32[12,96]{1,0:T(8,128)}, u32[]{:S(2)}) copy-start(f32[12,96]{1,0:T(8,128)} %param.31) | copy-start | bytes 13828
  12.4 35.9 %copy-start.39 = (s32[4,256]{1,0:T(4,128)S(1)}, s32[4,256]{1,0:T(4,128)}, u32[]{:S(2)}) copy-start(s32[4,256]{1,0:T(4,128)} %param.25) | copy-start | bytes 12292
  12.4 35.9 %copy-start.40 = (s32[4]{0:T(128)S(1)}, s32[4]{0:T(128)}, u32[]{:S(2)}) copy-start(s32[4]{0:T(128)} %param.26) | copy-start | bytes 52
  13.2 46.2 %collective-permute-start = (bf16[96,2304]{1,0:T(8,128)(2,1)}, bf16[96,2304]{1,0:T(8,128)(2,1)}, u32[]{:S(2)}, u32[]{:S(2)}) collective-permute-start(bf16[96,2304]{1,0:T(8,128)(2,1)} %get-tuple-element.257), channel_id=1, source_target_pairs={{0,1},{1,2},{2,3},{3,4},{4,5},{5,6},{6,7},{7,0},{8,9},{9,10},{10,1... | collective-permute-start | bytes 1327112 | tf_op jit(solution)/shard_map/ppermute | solution.py:29
  13.6 46.0 %collective-permute-start.1 = (bf16[96,2304]{1,0:T(8,128)(2,1)}, bf16[96,2304]{1,0:T(8,128)(2,1)}, u32[]{:S(2)}, u32[]{:S(2)}) collective-permute-start(bf16[96,2304]{1,0:T(8,128)(2,1)} %get-tuple-element.257), channel_id=1, source_target_pairs={{0,7},{1,0},{2,1},{3,2},{4,3},{5,4},{6,5},{7,6},{8,15},{9,8},{10,9... | collective-permute-start | bytes 1327112 | tf_op jit(solution)/shard_map/ppermute | solution.py:34
  19.8 324.3 %reduce-scatter.10.cloned.1.call-start = ((), (), s32[]{:S(2)}) async-start(), calls=%async_computation.9 | async-start | bytes 2654208 | tf_op jit(solution)/shard_map/reduce_scatter | solution.py:246
  57.7 58.5 %copy-start.6 = (bf16[1024,768]{1,0:T(8,128)(2,1)S(1)}, bf16[1024,768]{1,0:T(8,128)(2,1)}, u32[]{:S(2)}) copy-start(bf16[1024,768]{1,0:T(8,128)(2,1)} %param.23) | copy-start | bytes 4718596
  59.3 138.1 %copy-start.36 = (f32[768]{0:T(1024)}, f32[768]{0:T(1024)S(1)}, u32[]{:S(2)}) copy-start(f32[768]{0:T(1024)S(1)} %get-tuple-element.203) | copy-start | bytes 9220
  59.3 23.5 %collective-permute-start.2 = (bf16[96,2304]{1,0:T(8,128)(2,1)}, bf16[96,2304]{1,0:T(8,128)(2,1)S(1)}, u32[]{:S(2)}, u32[]{:S(2)}) collective-permute-start(bf16[96,2304]{1,0:T(8,128)(2,1)} %collective-permute-done), channel_id=1, source_target_pairs={{0,1},{1,2},{2,3},{3,4},{4,5},{5,6},{6,7},{7,0},{8,9},{9,10},{10,1... | collective-permute-start | bytes 1327112 | tf_op jit(solution)/shard_map/ppermute | solution.py:29
  59.7 23.2 %collective-permute-start.3 = (bf16[96,2304]{1,0:T(8,128)(2,1)}, bf16[96,2304]{1,0:T(8,128)(2,1)S(1)}, u32[]{:S(2)}, u32[]{:S(2)}) collective-permute-start(bf16[96,2304]{1,0:T(8,128)(2,1)} %collective-permute-done.1), channel_id=1, source_target_pairs={{0,7},{1,0},{2,1},{3,2},{4,3},{5,4},{6,5},{7,6},{8,15},{9,8},{10,9... | collective-permute-start | bytes 1327112 | tf_op jit(solution)/shard_map/ppermute | solution.py:34
  82.9 20.4 %collective-permute-start.4 = (bf16[96,2304]{1,0:T(8,128)(2,1)S(1)}, bf16[96,2304]{1,0:T(8,128)(2,1)S(1)}, u32[]{:S(2)}, u32[]{:S(2)}) collective-permute-start(bf16[96,2304]{1,0:T(8,128)(2,1)S(1)} %collective-permute-done.2), channel_id=1, source_target_pairs={{0,1},{1,2},{2,3},{3,4},{4,5},{5,6},{6,7},{7,0},{8,9},{9,10},{10,1... | collective-permute-start | bytes 1327112 | tf_op jit(solution)/shard_map/ppermute | solution.py:29
  82.9 22.5 %collective-permute-start.5 = (bf16[96,2304]{1,0:T(8,128)(2,1)S(1)}, bf16[96,2304]{1,0:T(8,128)(2,1)S(1)}, u32[]{:S(2)}, u32[]{:S(2)}) collective-permute-start(bf16[96,2304]{1,0:T(8,128)(2,1)S(1)} %collective-permute-done.3), channel_id=1, source_target_pairs={{0,7},{1,0},{2,1},{3,2},{4,3},{5,4},{6,5},{7,6},{8,15},{9,8},{10,9... | collective-permute-start | bytes 1327112 | tf_op jit(solution)/shard_map/ppermute | solution.py:34
  103.3 12.9 %collective-permute-start.6 = (bf16[96,2304]{1,0:T(8,128)(2,1)S(1)}, bf16[96,2304]{1,0:T(8,128)(2,1)S(1)}, u32[]{:S(2)}, u32[]{:S(2)}) collective-permute-start(bf16[96,2304]{1,0:T(8,128)(2,1)S(1)} %collective-permute-done.4), channel_id=1, source_target_pairs={{0,1},{1,2},{2,3},{3,4},{4,5},{5,6},{6,7},{7,0},{8,9},{9,10},{10,1... | collective-permute-start | bytes 1327112 | tf_op jit(solution)/shard_map/ppermute | solution.py:29
  131.2 5.5 copy-start.8
  158.5 38.8 %copy-start.1 = (f32[1024,768]{0,1:T(8,128)}, f32[1024,768]{0,1:T(8,128)S(1)}, u32[]{:S(2)}) copy-start(f32[1024,768]{0,1:T(8,128)S(1)} %get-tuple-element.268) | copy-start | bytes 9437188
  213.6 18.1 %copy-start.10 = (bf16[1024,768]{0,1:T(8,128)(2,1)}, bf16[1024,768]{0,1:T(8,128)(2,1)S(1)}, u32[]{:S(2)}) copy-start(bf16[1024,768]{0,1:T(8,128)(2,1)S(1)} %get-tuple-element.249) | copy-start | bytes 4718596
  231.7 11.2 %copy-start.2 = (f32[1024,768]{0,1:T(8,128)S(1)}, f32[1024,768]{0,1:T(8,128)}, u32[]{:S(2)}) copy-start(f32[1024,768]{0,1:T(8,128)} %copy-done.1) | copy-start | bytes 9437188
  254.0 139.1 %reduce-scatter.16.cloned.1.call-start = ((), (), s32[]{:S(2)}) async-start(), calls=%async_computation.12 | async-start | bytes 7962624
  289.4 8.8 %copy-start.7 = (bf16[1024,768]{1,0:T(8,128)(2,1)S(1)}, bf16[1024,768]{1,0:T(8,128)(2,1)}, u32[]{:S(2)}) copy-start(bf16[1024,768]{1,0:T(8,128)(2,1)} %param.23) | copy-start | bytes 4718596
  314.6 178.6 %reduce-scatter.14.cloned.1.call-start = ((), (), s32[]{:S(2)}) async-start(), calls=%async_computation.11 | async-start | bytes 10616832 | tf_op jit(solution)/shard_map/reduce_scatter | solution.py:248
  326.2 267.2 %reduce-scatter.12.cloned.1.call-start = ((), (), s32[]{:S(2)}) async-start(), calls=%async_computation.10 | async-start | bytes 10616832 | tf_op jit(solution)/shard_map/reduce_scatter | solution.py:247
  338.7 4.2 copy-start.29
  338.7 4.2 copy-start.28
  338.7 296.8 %all-gather.12.cloned.1.call-start = ((), (), s32[]{:S(2)}) async-start(), calls=%async_computation.8 | async-start | bytes 3981312 | tf_op jit(solution)/shard_map/all_gather | solution.py:188
  339.5 328.5 %reduce-scatter.18.cloned.1.call-start = ((), (), s32[]{:S(2)}) async-start(), calls=%async_computation.13 | async-start | bytes 442368
  344.0 394.5 %all-reduce.3.cloned.1.call-start = ((), (), s32[]{:S(2)}) async-start(), calls=%async_computation.14 | async-start | bytes 3833856 | tf_op jit(solution)/shard_map/psum | solution.py:252
  345.7 249.8 %copy-start.17 = (f32[96,2304]{1,0:T(8,128)S(1)}, f32[96,2304]{1,0:T(8,128)}, u32[]{:S(2)}) copy-start(f32[96,2304]{1,0:T(8,128)} %param.32) | copy-start | bytes 2654212
  644.8 34.3 %copy-start.34 = (f32[12,96]{1,0:T(8,128)S(1)}, f32[12,96]{1,0:T(8,128)}, u32[]{:S(2)}) copy-start(f32[12,96]{1,0:T(8,128)} %param.41) | copy-start | bytes 13828
  644.8 34.3 %copy-start.35 = (f32[12,96]{1,0:T(8,128)S(1)}, f32[12,96]{1,0:T(8,128)}, u32[]{:S(2)}) copy-start(f32[12,96]{1,0:T(8,128)} %param.36) | copy-start | bytes 13828
  (26 other events, 64.7 us)
Sparse Core Ops, SparseCore 0:
  10.2 29.1 all-gather.5
  41.6 68.3 all-gather.7
  112.2 53.3 all-gather.9
  254.1 37.3 reduce-scatter.9
  314.7 78.3 reduce-scatter.15
  395.3 97.8 reduce-scatter.13
  495.5 97.8 reduce-scatter.11
  595.6 39.8 all-gather.11
  638.4 29.5 reduce-scatter.17
  672.8 65.6 all-reduce.2
